TPU v7x, 256 devices: a whole 4x4x8 slice. The times are simulated.
256 devices in a mesh: clip: 16 (over z, core), seq: 16 (over x, y).
Axes of the slice: x: 4, y: 4, z: 8, core: 2. Of those that a mesh axis runs over, the one named last changes fastest.
Arguments:
- patches: bfloat16 [16, 10240, 1408], P('clip', 'seq'), may hold values from -6 to 6
- vis_index: int32 [16, 1024], P('clip'), may hold values from 0 to 10239, as said below
- enc_gain: float32 [1408], replicated, may hold values from 0.5 to 1.5
- w_qkv: bfloat16 [3, 1408, 1408], P(None, None, 'seq')
- w_out: bfloat16 [1408, 1408], P('seq'), may hold values from -2 to 2
- w_embed: bfloat16 [1408, 512], P(None, ('clip', 'seq')), may hold values from -0.15625 to 0.15625
- mask_token: bfloat16 [512], replicated, may hold values from -4 to 4
- pos_embed: bfloat16 [10240, 512], P('seq'), may hold values from -3 to 3
- dec_gain: float32 [512], replicated, may hold values from 0.5 to 1.5
- w_up: bfloat16 [512, 2048], P(None, ('clip', 'seq')), may hold values from -0.25 to 0.25
- w_down: bfloat16 [2048, 512], P(('clip', 'seq')), may hold values from -0.125 to 0.125
- w_pixel: bfloat16 [512, 1176], replicated, may hold values from -0.25 to 0.25
- target: bfloat16 [16, 10240, 1176], P('clip', 'seq'), may hold values from -6 to 6
Outputs:
- decoded: bfloat16 [16, 10240, 512], P('clip', 'seq')
- grad_pixel: float32 [16, 512, 1176], P('clip', 'seq')
Inputs may be any that keep to these rules, and one draw needn't show every extreme that they name: `vis_index`: strictly ascending within a clip. Among the 640 consecutive positions of any one index of seq at most 128 are visible, and in every clip some index holds exactly 128.
All inputs are finite; a program needn't handle non-finite values.
Results may differ from a plain program's by a relative error of at most 0.022.
The roundings to bfloat16 on the way count: a program that leaves them out, or rounds other values in their place, can miss the bound.
Values may be sent and summed in bfloat16 or wider, within the bound.
A program may use at most 64 MiB of HBM per device.

v0:
```python
import jax
import jax.numpy as jnp
from jax import lax
from jax.experimental import pallas as pl
from jax.experimental.pallas import tpu as pltpu
from jax.sharding import PartitionSpec as P

D = 1408
HEAD = 88
HPAD = 96
DEC = 512
HID = 2048
PIX = 1176
TOK = 640
CAP = 128
VIS = 1024
N = 16
ROWS = VIS // N
HALF = 768
F32 = jnp.float32
BF16 = jnp.bfloat16
MESH = pl.DeviceIdType.MESH
EXP_SCALE = HEAD ** (-0.5) * 1.4426950408889634

NT = (((1,), (1,)), ((), ()))
NN = (((1,), (0,)), ((), ()))
TN = (((0,), (0,)), ((), ()))
TT = (((0,), (1,)), ((), ()))


def dot(left, right, dims):
    return lax.dot_general(left, right, dims, preferred_element_type=F32)


def iota(shape, axis):
    return lax.broadcasted_iota(jnp.int32, shape, axis)


def norm_rows(values, gain):
    center = jnp.mean(values, axis=-1, keepdims=True)
    spread = jnp.mean((values - center) ** 2, axis=-1, keepdims=True)
    return ((values - center) * lax.rsqrt(spread + 1e-05) * gain).astype(BF16)


def rcopy(src, dst, send_sem, recv_sem, dev):
    return pltpu.make_async_remote_copy(
        src_ref=src,
        dst_ref=dst,
        send_sem=send_sem,
        recv_sem=recv_sem,
        device_id=dev,
        device_id_type=MESH,
    )


class PlaneGather:
    def __init__(self, buf, send, recv, clip, seq, cuts):
        self.buf, self.send, self.recv, self.clip = buf, send, recv, clip
        self.x, self.y = seq // 4, seq % 4
        self.cuts = cuts

    def rank(self, fam, p, q):
        dx, dy = (p, q) if fam == 0 else (q, p)
        return ((self.x + dx + 4) % 4) * 4 + (self.y + dy + 4) % 4

    def piece(self, fam, p, q, part):
        lo, mid, hi = self.cuts[fam]
        lo, hi = ((lo, hi), (lo, mid), (mid, hi))[part]
        return self.buf.at[self.rank(fam, p, q), pl.ds(lo, hi - lo)]

    def go(self, fam, p, q, part, to, stage):
        ref = self.piece(fam, p, q, part)
        dev = (self.clip, self.rank(fam, *to))
        rcopy(ref, ref, self.send, self.recv.at[stage], dev).start()

    def got(self, stage, pieces):
        ref = self.buf.at[pl.ds(0, pieces)]
        rcopy(ref, ref, self.send, self.recv.at[stage], (self.clip, self.rank(0, 1, 0))).wait_recv()

    def spread(self, fam, p):
        self.go(fam, p, 0, 0, (0, 1), 2 + p % 4)
        self.go(fam, p, 0, 0, (0, -1), 2 + p % 4)

    def first(self):
        for fam in (0, 1):
            self.go(fam, 0, 0, 0, (1, 0), 0)
            self.go(fam, 0, 0, 0, (-1, 0), 0)
        for fam in (0, 1):
            self.spread(fam, 0)

    def second(self):
        self.got(0, 2)
        for fam in (0, 1):
            self.go(fam, -1, 0, 1, (1, 0), 1)
            self.go(fam, 1, 0, 2, (-1, 0), 1)
        for fam in (0, 1):
            self.spread(fam, -1)
            self.spread(fam, 1)

    def third(self):
        self.got(1, 1)
        for fam in (0, 1):
            self.spread(fam, 2)

    def relay(self, p):
        self.got(2 + p % 4, 2)
        for fam in (0, 1):
            self.go(fam, p, -1, 1, (0, 1), 6 + p % 4)
            self.go(fam, p, 1, 2, (0, -1), 6 + p % 4)

    def last(self, p):
        self.got(6 + p % 4, 1)

    def finish(self):
        ref = self.buf.at[pl.ds(0, N - 1)]
        rcopy(ref, ref, self.send, self.recv.at[0], (self.clip, self.rank(0, 1, 0))).wait_send()


class LineGather:
    def __init__(self, buf, send, recv, side_send, side_recv, clip, seq, subs):
        self.buf, self.send, self.recv = buf, send, recv
        self.side_send, self.side_recv = side_send, side_recv
        self.clip, self.seq, self.subs = clip, seq, subs
        self.other = clip + 1 - 2 * (clip % 2)
        self.rows = buf.shape[1]

    def block(self, step):
        return (self.clip + 2 * step + 16) % 16

    def go(self, step, lo, size, way, sem):
        ref = self.buf.at[self.block(step), pl.ds(lo, size)]
        rcopy(ref, ref, self.send, self.recv.at[sem], (self.block(way), self.seq)).start()

    def got(self, sem, rows):
        ref = self.buf.at[0, pl.ds(0, rows)]
        rcopy(ref, ref, self.send, self.recv.at[sem], (self.block(1), self.seq)).wait_recv()

    def side(self, step):
        ref = self.buf.at[self.block(step)]
        rcopy(ref, ref, self.side_send, self.side_recv, (self.other, self.seq)).start()

    def step(self, t, sub=0):
        size = self.rows // self.subs
        sem = t * self.subs + sub
        half = self.rows // 2
        done = sub == self.subs - 1
        if t == 0:
            self.go(0, sub * size, size, 1, sem)
            self.go(0, sub * size, size, -1, sem)
            if done:
                self.side(0)
        elif t == 4:
            self.got(sem - self.subs, half if self.subs == 2 else self.rows)
            if done:
                self.side(4)
        else:
            both = self.buf.at[pl.ds(0, 2), pl.ds(0, size)]
            rcopy(
                both, both, self.send, self.recv.at[sem - self.subs], (self.block(1), self.seq)
            ).wait_recv()
            if t < 3:
                self.go(-t, sub * size, size, 1, sem)
                self.go(t, sub * size, size, -1, sem)
            else:
                if sub == 0:
                    self.go(-3, 0, half, 1, sem)
                if done:
                    self.go(3, half, half, -1, sem)
            if done:
                self.side(-t)
                self.side(t)

    def sides(self):
        ref = self.buf.at[pl.ds(0, 8)]
        rcopy(ref, ref, self.side_send, self.side_recv, (self.other, self.seq)).wait_recv()

    def finish(self):
        ref = self.buf.at[pl.ds(0, 7)]
        rcopy(ref, ref, self.send, self.recv.at[0], (self.block(1), self.seq)).wait_send()
        ref = self.buf.at[pl.ds(0, 8)]
        rcopy(ref, ref, self.side_send, self.side_recv, (self.other, self.seq)).wait_send()


def kernel(
    patches,
    vis,
    enc_gain,
    w_qkv,
    w_out,
    w_embed,
    mask_token,
    pos_embed,
    dec_gain,
    w_up,
    w_down,
    w_pixel,
    target,
    decoded_out,
    grad_out,
    patch_v,
    pos_v,
    pix_v,
    tgt_v,
    ud_mine,
    e_mine,
    pick_v,
    seen_v,
    visible_v,
    row_send,
    row_recv,
    rows_v,
    code_v,
    qv_v,
    keys_v,
    ho_v,
    ho_send,
    ho_recv,
    wo_v,
    ud_v,
    e_v,
    up_v,
    down_v,
    emb_v,
    acc_v,
    dec_v,
    dn_v,
    g_send,
    g_recv,
    g_mid,
    g_last,
    load_sem,
    ud_s,
    e_s,
    a2a_s,
    ho_s,
    g_s,
    wside_s,
    ag_s,
    ag_r,
    wo_s,
    wo_r,
    zu_s,
    zu_r,
    ze_s,
    ze_r,
):
    clip, seq = lax.axis_index("clip"), lax.axis_index("seq")
    core = clip % 2
    other = clip + 1 - 2 * core

    loads = [
        pltpu.make_async_copy(src, dst, load_sem.at[i])
        for i, (src, dst) in enumerate(
            ((patches, patch_v), (pos_embed, pos_v), (w_pixel, pix_v), (target, tgt_v))
        )
    ]
    for load in loads:
        load.start()

    barrier = pltpu.get_barrier_semaphore()

    @pl.loop(1, N)
    def _(o):
        pl.semaphore_signal(
            barrier, inc=1, device_id=(clip, (seq + o) % N), device_id_type=MESH
        )

    for dev in (other, (clip + 2) % 16, (clip + 14) % 16):
        pl.semaphore_signal(barrier, inc=1, device_id=(dev, seq), device_id_type=MESH)

    ud_mine[...] = jnp.concatenate(
        [w_up[...].astype(F32), w_down[...].astype(F32)], axis=0
    ).astype(BF16)
    emb_rows = jnp.concatenate([w_embed[...].astype(F32), jnp.zeros((2, 128), F32)], axis=1)
    packed = jnp.zeros((16, 256), F32)
    row16 = iota((16, 256), 0)
    for a in range(2):
        for q in range(6):
            line = jnp.broadcast_to(emb_rows[a : a + 1, q * 256 : (q + 1) * 256], (16, 256))
            packed = jnp.where(row16 == a * 8 + q, line, packed)
    e_mine[...] = packed.astype(BF16)
    my16 = pl.ds(pl.multiple_of(seq * 16, 16), 16)
    ud_v[clip, my16, :] = ud_mine[...]
    e_v[clip, my16, :] = e_mine[...]

    def all_peers(copy):
        @pl.loop(1, N)
        def _(o):
            copy((seq + o) % N).start()

    next_dev = (clip, (seq + 1) % N)

    def both(src, dst, sems):
        return rcopy(src, dst, sems.at[0], sems.at[1], next_dev)

    def ud_copy(peer):
        return rcopy(ud_mine, ud_v.at[clip, my16], ud_s.at[0], ud_s.at[1], (clip, peer))

    def e_copy(peer):
        return rcopy(e_mine, e_v.at[clip, my16], e_s.at[0], e_s.at[1], (clip, peer))

    def a2a_copy(peer):
        return rcopy(row_send.at[peer], row_recv.at[seq], a2a_s.at[0], a2a_s.at[1], (clip, peer))

    def ho_copy(peer):
        return rcopy(ho_send.at[peer], ho_recv.at[seq], ho_s.at[0], ho_s.at[1], (clip, peer))

    many = pl.ds(0, N - 1)
    ud_all = ud_v.at[clip, pl.ds(0, 16 * (N - 1))]
    e_all = e_v.at[clip, pl.ds(0, 16 * (N - 1))]
    ud_wait = both(ud_all, ud_all, ud_s)
    e_wait = both(e_all, e_all, e_s)
    a2a_wait = both(row_send.at[many], row_recv.at[many], a2a_s)
    ho_wait = both(ho_send.at[many], ho_recv.at[many], ho_s)

    token = vis[...]
    here = iota((ROWS, VIS), 1) // N == iota((ROWS, VIS), 0)
    column = (iota((VIS, N), 0) % N == iota((VIS, N), 1)).astype(F32).astype(BF16)

    def digit(values):
        spread = jnp.where(here, jnp.broadcast_to(values, (ROWS, VIS)), 0)
        return dot(spread.astype(F32).astype(BF16), column, NN)

    v64 = (digit(token // 128) * 128.0 + digit(token % 128)).astype(jnp.int32)
    own64 = jnp.zeros((ROWS, N), jnp.int32)
    for d in range(1, N):
        own64 = own64 + (v64 >= d * TOK).astype(jnp.int32)
    mine = jnp.where(own64 == seq, v64 - seq * TOK + 1, 0)
    place = mine[0:8]
    for a in range(1, 8):
        place = place + mine[8 * a : 8 * a + 8]
    spot = jnp.concatenate([place[:, j : j + 1] for j in range(N)], axis=0) - 1
    pick = (iota((CAP, TOK), 1) == spot).astype(F32)
    seen_v[...] = jnp.sum(pick, axis=0, keepdims=True)
    pick_v[...] = pick.astype(BF16)
    loads[0].wait()
    visible = dot(pick_v[...], patch_v[...], NN)
    visible_v[...] = visible
    center = jnp.mean(visible, axis=-1, keepdims=True)
    spread = jnp.mean((visible - center) ** 2, axis=-1, keepdims=True)
    normed = (visible - center) * lax.rsqrt(spread + 1e-05) * enc_gain[...].reshape(1, D)
    for j in range(N):
        row_send[j] = normed[8 * j : 8 * j + 8].astype(BF16)
    row_recv[seq] = row_send[seq]

    pl.semaphore_wait(barrier, N - 1 + 3)
    all_peers(ud_copy)
    all_peers(a2a_copy)

    line_ud = LineGather(ud_v, zu_s.at[0], zu_r, zu_s.at[1], zu_s.at[2], clip, seq, 2)
    line_e = LineGather(e_v, ze_s.at[0], ze_r, ze_s.at[1], ze_s.at[2], clip, seq, 1)
    ud_wait.wait_recv()
    line_ud.step(0, 0)
    line_ud.step(0, 1)

    low = iota((ROWS, 1), 0) % 8
    for j in range(N):
        code = own64[:, j : j + 1] * CAP + j * 8 + low
        code_v[j * ROWS : (j + 1) * ROWS, :] = (
            (iota((ROWS, N * CAP), 1) == code).astype(F32).astype(BF16)
        )

    own_me = jnp.sum(
        jnp.where(iota((ROWS, N), 1) == seq, own64, 0), axis=1, keepdims=True
    )
    lane = iota((ROWS, N * 8), 1)
    gather = ((own_me == lane // 8) & (low == lane % 8)).astype(F32).astype(BF16)
    a2a_wait.wait_recv()
    arrived = jnp.concatenate([row_recv[d].astype(F32) for d in range(N)], axis=0).astype(BF16)
    rows_v[seq] = dot(gather, arrived, NN).astype(BF16)
    rows_ag = PlaneGather(rows_v, ag_s, ag_r, clip, seq, ((0, 16, 32), (32, 48, 64)))
    rows_ag.first()
    all_peers(e_copy)

    wide = jnp.concatenate([w_out[...].astype(F32), jnp.zeros((HPAD - HEAD, D), F32)], axis=0)
    wo_v[0, seq] = wide[:, :HALF].astype(BF16)
    wo_v[1, seq] = jnp.concatenate(
        [wide[:, HALF:], jnp.zeros((HPAD, 2 * HALF - D), F32)], axis=1
    ).astype(BF16)
    wo_ag = PlaneGather(wo_v.at[core], wo_s, wo_r, clip, seq, ((0, 32, 48), (48, 80, 96)))

    line_ud.step(1, 0)
    rows_ag.second()

    loads[1].wait()
    dec_masked = (mask_token[...].astype(F32).reshape(1, DEC) + pos_v[...].astype(F32)).astype(BF16)

    def mlp_start(dec_in, count):
        acc_v[0:count, :] = dec_in.astype(F32)
        dn_v[0:count, :] = norm_rows(dec_in.astype(F32), dec_gain[...].reshape(1, DEC))

    mlp_start(dec_masked, TOK)
    line_ud.step(1, 1)
    rows_ag.third()

    r256, c256 = iota((256, 256), 0), iota((256, 256), 1)
    unit = r256 % 128
    order_ud = (c256 == (unit // 8) * 16 + unit % 8 + 8 * (r256 // 128)).astype(F32).astype(BF16)
    r192, c192 = iota((192, 256), 0), iota((192, 256), 1)
    order_e = (c192 == (r192 % 32) * 8 + r192 // 32).astype(F32).astype(BF16)

    def sort_ud(b):
        two = dot(order_ud, ud_v[b], NN).astype(BF16)
        at = pl.ds(pl.multiple_of(b * 128, 128), 128)
        up_v[at, :] = two[:128]
        down_v[at, :] = two[128:]

    def sort_e(b):
        lines = dot(order_e, e_v[b], NN).astype(BF16)
        at = pl.ds(pl.multiple_of(b * 32, 32), 32)
        for q in range(6):
            emb_v[at, q * 256 : (q + 1) * 256] = lines[q * 32 : (q + 1) * 32]

    line_ud.step(2, 0)
    for t in (0, -1, 1):
        sort_ud(line_ud.block(t))
    rows_ag.relay(0)
    line_ud.step(2, 1)
    rows_ag.relay(-1)
    for t in (-2, 2):
        sort_ud(line_ud.block(t))
    line_ud.step(3, 0)
    rows_ag.relay(1)
    line_ud.step(3, 1)
    rows_ag.relay(2)
    wo_ag.first()
    for t in (-3, 3):
        sort_ud(line_ud.block(t))
    for p in (0, -1, 1, 2):
        rows_ag.last(p)
    line_ud.step(4, 0)
    line_ud.step(4, 1)
    e_wait.wait_recv()
    line_e.step(0)

    zeros_q = jnp.zeros((HPAD - HEAD, 256), F32)
    zeros_k = jnp.zeros((256, HPAD - HEAD), F32)

    def project(b):
        rows = rows_v[4 * b : 4 * b + 4].reshape(256, D)
        at = pl.ds(b * 256, 256)
        for i, top in ((0, 0), (2, HPAD)):
            part = dot(w_qkv[i], rows, NT)
            qv_v[pl.ds(top, HPAD), at] = jnp.concatenate([part, zeros_q], axis=0).astype(BF16)
        keys = dot(rows, w_qkv[1], NT)
        keys_v[at, :] = jnp.concatenate([keys, zeros_k], axis=1).astype(BF16)

    def attend(b):
        at = pl.ds(b * 256, 256)
        scores = dot(keys_v[...], qv_v[pl.ds(0, HPAD), at], NN)
        peak = jnp.max(scores, axis=0, keepdims=True)
        expo = jnp.exp2((scores - peak) * EXP_SCALE)
        total = jnp.sum(expo, axis=0, keepdims=True)
        probs = (expo * (1.0 / total)).astype(BF16)
        ho_v[:, at] = dot(qv_v[pl.ds(HPAD, HPAD), :], probs, NN).astype(BF16)

    project(0)
    project(1)
    wo_ag.second()
    project(2)
    project(3)
    wo_ag.third()
    attend(0)
    line_e.step(1)
    attend(1)
    wo_ag.relay(0)
    attend(2)
    wo_ag.relay(-1)
    attend(3)

    @pl.loop(0, N // 2, unroll=4)
    def _(h):
        two = dot(
            ho_v[...], code_v[:, pl.ds(pl.multiple_of(h * 256, 256), 256)], NN
        ).astype(BF16)
        ho_send[2 * h] = two[:, :CAP]
        ho_send[2 * h + 1] = two[:, CAP:]

    ho_recv[seq] = ho_send[seq]
    all_peers(ho_copy)
    line_e.step(2)
    sort_ud(line_ud.block(4))
    line_ud.sides()

    @pl.loop(0, 8, unroll=4)
    def _(t):
        sort_ud((other + 2 * t) % 16)

    def mlp(count):
        @pl.loop(0, 4, unroll=2)
        def _(h):
            at = pl.ds(pl.multiple_of(h * 512, 512), 512)
            hidden = jax.nn.gelu(dot(dn_v[0:count, :], up_v[at, :], NT)).astype(BF16)
            acc_v[0:count, :] += dot(hidden, down_v[at, :], NN)

        return acc_v[0:count, :].astype(BF16)

    dec_v[...] = mlp(TOK)
    line_e.step(3)
    wo_ag.relay(1)
    wo_ag.relay(2)
    loads[2].wait()
    loads[3].wait()
    keep = 1.0 - seen_v[...]

    x, y = seq // 4, seq % 4
    first_at, second_at = (x, y), (y, x)

    def plane_dev(fam, p, q):
        return (clip, p * 4 + q if fam == 0 else q * 4 + p)

    def g_first(fam, o):
        p, q = first_at[fam], second_at[fam]
        to = (p + o) % 4
        return rcopy(
            g_send.at[fam, pl.ds(to * 4, 4)],
            g_recv.at[fam, p],
            g_s.at[fam, 0],
            g_s.at[fam, 1],
            plane_dev(fam, to, q),
        )

    def g_second(fam, o):
        p, q = first_at[fam], second_at[fam]
        to = (q + o) % 4
        return rcopy(
            g_mid.at[fam, to],
            g_last.at[fam, q],
            g_s.at[fam, 2],
            g_s.at[fam, 3],
            plane_dev(fam, p, to),
        )

    for fam, (lo, hi) in enumerate(((0, 640), (640, PIX))):
        predicted = dot(pix_v[lo:hi, :], dec_v[...], NT)
        resid = ((predicted - tgt_v[lo:hi, :].astype(F32)) * keep).astype(BF16)
        for quarter in range(4):
            term = dot(dec_v[:, quarter * 128 : (quarter + 1) * 128], resid, TT) * (2.0 / PIX)
            if hi - lo < 640:
                term = jnp.concatenate([term, jnp.zeros((128, 640 - hi + lo), F32)], axis=1)
            for i in range(4):
                spot_g = quarter * 4 + i if fam == 0 else i * 4 + quarter
                g_send[fam, spot_g] = term[32 * i : 32 * i + 32].astype(BF16)
        for o in (1, 2, 3):
            g_first(fam, o).start()

    for p in (0, -1, 1, 2):
        wo_ag.last(p)

    def wo_side(j):
        ref = wo_v.at[core, j]
        return rcopy(ref, ref, wside_s.at[0], wside_s.at[1], (other, seq))

    wo_rest = wo_v.at[0, many]
    wo_wait = rcopy(wo_rest, wo_rest, wside_s.at[0], wside_s.at[1], (other, seq))
    all_peers(wo_side)
    line_e.step(4)
    line_e.sides()

    @pl.loop(0, N, unroll=4)
    def _(b):
        sort_e(b)

    pos_rows = dot(pick_v[...], pos_v[...], NN)

    ho_wait.wait_recv()
    wo_wait.wait_recv()
    heads = ho_recv[...].reshape(N * HPAD, CAP)
    attended = jnp.concatenate(
        [dot(heads, wo_v[half].reshape(N * HPAD, HALF), TN) for half in range(2)], axis=1
    )
    encoded = (visible_v[...] + attended[:, :D]).astype(BF16)
    embedded = dot(encoded, emb_v[:, :D], NT).astype(BF16)
    mlp_start((embedded.astype(F32) + pos_rows).astype(BF16), CAP)

    for fam in (0, 1):
        p, q = first_at[fam], second_at[fam]
        three = pl.ds(0, 3)
        rcopy(
            g_recv.at[fam, three], g_recv.at[fam, three], g_s.at[fam, 0], g_s.at[fam, 1], next_dev
        ).wait_recv()
        part = g_send[fam, pl.ds(p * 4, 4)].astype(F32)
        for o in (1, 2, 3):
            part = part + g_recv[fam, (p + o) % 4].astype(F32)
        g_mid[fam] = part.astype(BF16)
        for o in (1, 2, 3):
            g_second(fam, o).start()

    vis_dec = mlp(CAP)
    pick_dot = dot(pick_v[...], vis_dec, TN)
    seen_col = dot(pick_v[...], jnp.ones((CAP, DEC), BF16), TN)
    decoded_out[...] = jnp.where(seen_col > 0.5, pick_dot, dec_v[...].astype(F32)).astype(BF16)

    sums = []
    for fam in (0, 1):
        p, q = first_at[fam], second_at[fam]
        three = pl.ds(0, 3)
        rcopy(
            g_last.at[fam, three], g_last.at[fam, three], g_s.at[fam, 2], g_s.at[fam, 3], next_dev
        ).wait_recv()
        total = g_mid[fam, q].astype(F32)
        for o in (1, 2, 3):
            total = total + g_last[fam, (q + o) % 4].astype(F32)
        sums.append(total)
    grad_out[...] = jnp.concatenate(sums, axis=1)[:, :PIX]

    for made in (ud_wait, e_wait, a2a_wait, ho_wait, wo_wait):
        made.wait_send()
    for fam in (0, 1):
        three = pl.ds(0, 3)
        rcopy(
            g_recv.at[fam, three], g_recv.at[fam, three], g_s.at[fam, 0], g_s.at[fam, 1], next_dev
        ).wait_send()
        rcopy(
            g_last.at[fam, three], g_last.at[fam, three], g_s.at[fam, 2], g_s.at[fam, 3], next_dev
        ).wait_send()
    rows_ag.finish()
    wo_ag.finish()
    line_ud.finish()
    line_e.finish()


def shards(
    patches,
    vis_index,
    enc_gain,
    w_qkv,
    w_out,
    w_embed,
    mask_token,
    pos_embed,
    dec_gain,
    w_up,
    w_down,
    w_pixel,
    target,
):
    vmem = pl.BlockSpec(memory_space=pltpu.VMEM)
    hbm = pl.BlockSpec(memory_space=pl.ANY)
    dma = pltpu.SemaphoreType.DMA
    decoded, grad = pl.pallas_call(
        kernel,
        out_shape=(
            jax.ShapeDtypeStruct((TOK, DEC), BF16),
            jax.ShapeDtypeStruct((DEC // N, PIX), F32),
        ),
        in_specs=[hbm, vmem, vmem, vmem, vmem, vmem, vmem, hbm, vmem, vmem, vmem, hbm, hbm],
        out_specs=(vmem, vmem),
        scratch_shapes=[
            pltpu.VMEM((TOK, D), BF16),
            pltpu.VMEM((TOK, DEC), BF16),
            pltpu.VMEM((PIX, DEC), BF16),
            pltpu.VMEM((PIX, TOK), BF16),
            pltpu.VMEM((16, 512), BF16),
            pltpu.VMEM((16, 256), BF16),
            pltpu.VMEM((CAP, TOK), BF16),
            pltpu.VMEM((1, TOK), F32),
            pltpu.VMEM((CAP, D), F32),
            pltpu.VMEM((N, 8, D), BF16),
            pltpu.VMEM((N, 8, D), BF16),
            pltpu.VMEM((N, ROWS, D), BF16),
            pltpu.VMEM((VIS, N * CAP), BF16),
            pltpu.VMEM((2 * HPAD, VIS), BF16),
            pltpu.VMEM((VIS, HPAD), BF16),
            pltpu.VMEM((HPAD, VIS), BF16),
            pltpu.VMEM((N, HPAD, CAP), BF16),
            pltpu.VMEM((N, HPAD, CAP), BF16),
            pltpu.VMEM((2, N, HPAD, HALF), BF16),
            pltpu.VMEM((N, 256, 512), BF16),
            pltpu.VMEM((N, 256, 256), BF16),
            pltpu.VMEM((HID, DEC), BF16),
            pltpu.VMEM((HID, DEC), BF16),
            pltpu.VMEM((DEC, 2 * HALF), BF16),
            pltpu.VMEM((TOK, DEC), F32),
            pltpu.VMEM((TOK, DEC), BF16),
            pltpu.VMEM((TOK, DEC), BF16),
            pltpu.VMEM((2, N, 32, 640), BF16),
            pltpu.VMEM((2, 4, 4, 32, 640), BF16),
            pltpu.VMEM((2, 4, 32, 640), BF16),
            pltpu.VMEM((2, 4, 32, 640), BF16),
            dma((4,)),
            dma((2,)),
            dma((2,)),
            dma((2,)),
            dma((2,)),
            dma((2, 4)),
            dma((2,)),
            dma,
            dma((10,)),
            dma,
            dma((10,)),
            dma((3,)),
            dma((8,)),
            dma((3,)),
            dma((4,)),
        ],
        compiler_params=pltpu.CompilerParams(
            collective_id=0, has_side_effects=True, vmem_limit_bytes=60 * 1024 * 1024
        ),
    )(
        patches[0],
        vis_index,
        enc_gain,
        jnp.transpose(w_qkv, (0, 2, 1)),
        w_out,
        w_embed.T,
        mask_token,
        pos_embed,
        dec_gain,
        w_up.T,
        w_down,
        w_pixel.T,
        target[0].T,
    )
    return decoded[None], grad[None]


def solution(mesh):
    placed = (
        P("clip", "seq", None),
        P("clip", None),
        P(),
        P(None, None, "seq"),
        P("seq", None),
        P(None, ("clip", "seq")),
        P(),
        P("seq", None),
        P(),
        P(None, ("clip", "seq")),
        P(("clip", "seq"), None),
        P(),
        P("clip", "seq", None),
    )
    return jax.shard_map(
        shards,
        mesh=mesh,
        in_specs=placed,
        out_specs=(P("clip", "seq", None), P("clip", "seq", None)),
        check_vma=False,
    )
```

profile of v0, /device:TPU:1, one launch (start us, length us, event | category | flops | bytes accessed | tf_op | source)
XLA Modules:
  0.0 82.8 jit_solution(3737750511310018787)
XLA Ops:
  0.6 78.6 %shard_map.140 = (bf16[640,512]{1,0:T(8,128)(2,1)}, f32[32,1176]{1,0:T(8,128)}) custom-call(bf16[640,1408]{1,0:T(8,128)(2,1)} %bitcast.10, s32[1,1024]{1,0:T(1,128)} %vis.1, f32[1408]{0:T(1024)} %enc_gain.1, bf16[3,88,1408]{2,1,0:T(8,128)(2,1)} %bitcast.13, bf16[88,1408]{1,0:T(8,128)(2,1)} %w_out.1, bf16[2,1408]{1,0:T(2,128)(2,1)} %bitcast.17, ...), custom_call_target="tpu_custom_call" | custom-call | tf_op jit(solution)/shard_map/pallas_call | solution.py:641
  79.3 2.0 %copy.17 = bf16[1,640,512]{2,1,0:T(8,128)(2,1)} copy(bf16[1,640,512]{2,1,0:T(8,128)(2,1)} %bitcast.14) | data formatting | bytes 1310720
  81.3 1.6 %copy.18 = f32[1,32,1176]{2,1,0:T(8,128)} copy(f32[1,32,1176]{2,1,0:T(8,128)} %bitcast.15) | data formatting | bytes 301056
where the time goes:
time: 83 us; the launch traced here: 82.8 us
  Pallas kernels  78.6 us (95%)
  local copies, waits for them, and re-layouts  3.56 us (4%)
    pallas_call x1, Pallas kernels, shards(): pl.pallas_call(kernel, out_shape=(jax.ShapeDtypeStruct((TOK, DEC), BF16),...  78.6 us
    unnamed x2, local copies, waits for them, and re-layouts  3.56 us

commit v1 on v0

--- a/solution.py
+++ b/solution.py
@@ -195,8 +195,10 @@
     w_down,
     w_pixel,
     target,
-    decoded_out,
-    grad_out,
+    dec_out,
+    vis_out,
+    pick_out,
+    sum_out,
     patch_v,
     pos_v,
     pix_v,
@@ -343,9 +345,17 @@
         row_send[j] = normed[8 * j : 8 * j + 8].astype(BF16)
     row_recv[seq] = row_send[seq]
 
+    wide = jnp.concatenate([w_out[...].astype(F32), jnp.zeros((HPAD - HEAD, D), F32)], axis=0)
+    wo_v[0, seq] = wide[:, :HALF].astype(BF16)
+    wo_v[1, seq] = jnp.concatenate(
+        [wide[:, HALF:], jnp.zeros((HPAD, 2 * HALF - D), F32)], axis=1
+    ).astype(BF16)
+    wo_ag = PlaneGather(wo_v.at[core], wo_s, wo_r, clip, seq, ((0, 32, 48), (48, 80, 96)))
+
     pl.semaphore_wait(barrier, N - 1 + 3)
     all_peers(ud_copy)
     all_peers(a2a_copy)
+    wo_ag.first()
 
     line_ud = LineGather(ud_v, zu_s.at[0], zu_r, zu_s.at[1], zu_s.at[2], clip, seq, 2)
     line_e = LineGather(e_v, ze_s.at[0], ze_r, ze_s.at[1], ze_s.at[2], clip, seq, 1)
@@ -370,14 +380,6 @@
     rows_v[seq] = dot(gather, arrived, NN).astype(BF16)
     rows_ag = PlaneGather(rows_v, ag_s, ag_r, clip, seq, ((0, 16, 32), (32, 48, 64)))
     rows_ag.first()
-    all_peers(e_copy)
-
-    wide = jnp.concatenate([w_out[...].astype(F32), jnp.zeros((HPAD - HEAD, D), F32)], axis=0)
-    wo_v[0, seq] = wide[:, :HALF].astype(BF16)
-    wo_v[1, seq] = jnp.concatenate(
-        [wide[:, HALF:], jnp.zeros((HPAD, 2 * HALF - D), F32)], axis=1
-    ).astype(BF16)
-    wo_ag = PlaneGather(wo_v.at[core], wo_s, wo_r, clip, seq, ((0, 32, 48), (48, 80, 96)))
 
     line_ud.step(1, 0)
     rows_ag.second()
@@ -414,24 +416,22 @@
     line_ud.step(2, 0)
     for t in (0, -1, 1):
         sort_ud(line_ud.block(t))
+    wo_ag.second()
     rows_ag.relay(0)
     line_ud.step(2, 1)
     rows_ag.relay(-1)
+    wo_ag.third()
     for t in (-2, 2):
         sort_ud(line_ud.block(t))
     line_ud.step(3, 0)
     rows_ag.relay(1)
     line_ud.step(3, 1)
     rows_ag.relay(2)
-    wo_ag.first()
+    all_peers(e_copy)
     for t in (-3, 3):
         sort_ud(line_ud.block(t))
     for p in (0, -1, 1, 2):
         rows_ag.last(p)
-    line_ud.step(4, 0)
-    line_ud.step(4, 1)
-    e_wait.wait_recv()
-    line_e.step(0)
 
     zeros_q = jnp.zeros((HPAD - HEAD, 256), F32)
     zeros_k = jnp.zeros((256, HPAD - HEAD), F32)
@@ -455,30 +455,15 @@
         ho_v[:, at] = dot(qv_v[pl.ds(HPAD, HPAD), :], probs, NN).astype(BF16)
 
     project(0)
+    line_ud.step(4, 0)
+    wo_ag.relay(0)
     project(1)
-    wo_ag.second()
+    line_ud.step(4, 1)
+    e_wait.wait_recv()
+    line_e.step(0)
     project(2)
+    wo_ag.relay(-1)
     project(3)
-    wo_ag.third()
-    attend(0)
-    line_e.step(1)
-    attend(1)
-    wo_ag.relay(0)
-    attend(2)
-    wo_ag.relay(-1)
-    attend(3)
-
-    @pl.loop(0, N // 2, unroll=4)
-    def _(h):
-        two = dot(
-            ho_v[...], code_v[:, pl.ds(pl.multiple_of(h * 256, 256), 256)], NN
-        ).astype(BF16)
-        ho_send[2 * h] = two[:, :CAP]
-        ho_send[2 * h + 1] = two[:, CAP:]
-
-    ho_recv[seq] = ho_send[seq]
-    all_peers(ho_copy)
-    line_e.step(2)
     sort_ud(line_ud.block(4))
     line_ud.sides()
 
@@ -486,19 +471,19 @@
     def _(t):
         sort_ud((other + 2 * t) % 16)
 
-    def mlp(count):
-        @pl.loop(0, 4, unroll=2)
-        def _(h):
-            at = pl.ds(pl.multiple_of(h * 512, 512), 512)
-            hidden = jax.nn.gelu(dot(dn_v[0:count, :], up_v[at, :], NT)).astype(BF16)
-            acc_v[0:count, :] += dot(hidden, down_v[at, :], NN)
-
-        return acc_v[0:count, :].astype(BF16)
-
-    dec_v[...] = mlp(TOK)
-    line_e.step(3)
+    def mlp_part(count, h):
+        at = pl.ds(h * 512, 512)
+        hidden = jax.nn.gelu(dot(dn_v[0:count, :], up_v[at, :], NT)).astype(BF16)
+        acc_v[0:count, :] += dot(hidden, down_v[at, :], NN)
+
+    mlp_part(TOK, 0)
     wo_ag.relay(1)
+    mlp_part(TOK, 1)
+    mlp_part(TOK, 2)
     wo_ag.relay(2)
+    mlp_part(TOK, 3)
+    dec_v[...] = acc_v[...].astype(BF16)
+    line_e.step(1)
     loads[2].wait()
     loads[3].wait()
     keep = 1.0 - seen_v[...]
@@ -544,6 +529,7 @@
         for o in (1, 2, 3):
             g_first(fam, o).start()
 
+    line_e.step(2)
     for p in (0, -1, 1, 2):
         wo_ag.last(p)
 
@@ -554,25 +540,23 @@
     wo_rest = wo_v.at[0, many]
     wo_wait = rcopy(wo_rest, wo_rest, wside_s.at[0], wside_s.at[1], (other, seq))
     all_peers(wo_side)
+    attend(0)
+    attend(1)
+    line_e.step(3)
+    attend(2)
+    attend(3)
+
+    @pl.loop(0, N // 2, unroll=4)
+    def _(h):
+        two = dot(
+            ho_v[...], code_v[:, pl.ds(pl.multiple_of(h * 256, 256), 256)], NN
+        ).astype(BF16)
+        ho_send[2 * h] = two[:, :CAP]
+        ho_send[2 * h + 1] = two[:, CAP:]
+
+    ho_recv[seq] = ho_send[seq]
+    all_peers(ho_copy)
     line_e.step(4)
-    line_e.sides()
-
-    @pl.loop(0, N, unroll=4)
-    def _(b):
-        sort_e(b)
-
-    pos_rows = dot(pick_v[...], pos_v[...], NN)
-
-    ho_wait.wait_recv()
-    wo_wait.wait_recv()
-    heads = ho_recv[...].reshape(N * HPAD, CAP)
-    attended = jnp.concatenate(
-        [dot(heads, wo_v[half].reshape(N * HPAD, HALF), TN) for half in range(2)], axis=1
-    )
-    encoded = (visible_v[...] + attended[:, :D]).astype(BF16)
-    embedded = dot(encoded, emb_v[:, :D], NT).astype(BF16)
-    mlp_start((embedded.astype(F32) + pos_rows).astype(BF16), CAP)
-
     for fam in (0, 1):
         p, q = first_at[fam], second_at[fam]
         three = pl.ds(0, 3)
@@ -586,10 +570,30 @@
         for o in (1, 2, 3):
             g_second(fam, o).start()
 
-    vis_dec = mlp(CAP)
-    pick_dot = dot(pick_v[...], vis_dec, TN)
-    seen_col = dot(pick_v[...], jnp.ones((CAP, DEC), BF16), TN)
-    decoded_out[...] = jnp.where(seen_col > 0.5, pick_dot, dec_v[...].astype(F32)).astype(BF16)
+    line_e.sides()
+
+    @pl.loop(0, N, unroll=4)
+    def _(b):
+        sort_e(b)
+
+    pos_rows = dot(pick_v[...], pos_v[...], NN)
+
+    ho_wait.wait_recv()
+    wo_wait.wait_recv()
+    heads = ho_recv[...].reshape(N * HPAD, CAP)
+    attended = jnp.concatenate(
+        [dot(heads, wo_v[half].reshape(N * HPAD, HALF), TN) for half in range(2)], axis=1
+    )
+    encoded = (visible_v[...] + attended[:, :D]).astype(BF16)
+    embedded = dot(encoded, emb_v[:, :D], NT).astype(BF16)
+    mlp_start((embedded.astype(F32) + pos_rows).astype(BF16), CAP)
+
+    for h in range(4):
+        mlp_part(CAP, h)
+    vis_dec = acc_v[0:CAP, :].astype(BF16)
+    dec_out[...] = dec_v[...]
+    vis_out[...] = vis_dec
+    pick_out[...] = pick_v[...]
 
     sums = []
     for fam in (0, 1):
@@ -602,7 +606,7 @@
         for o in (1, 2, 3):
             total = total + g_last[fam, (q + o) % 4].astype(F32)
         sums.append(total)
-    grad_out[...] = jnp.concatenate(sums, axis=1)[:, :PIX]
+    sum_out[...] = jnp.concatenate(sums, axis=1)[:, :PIX]
 
     for made in (ud_wait, e_wait, a2a_wait, ho_wait, wo_wait):
         made.wait_send()
@@ -618,6 +622,28 @@
     wo_ag.finish()
     line_ud.finish()
     line_e.finish()
+
+
+def merge(
+    dec_in, vis_in, pick_in, total_in, decoded_out, grad_out, dec, vis_dec, pick, total, sems
+):
+    moves = [
+        pltpu.make_async_copy(src, dst, sems.at[i])
+        for i, (src, dst) in enumerate(
+            ((pick_in, pick), (vis_in, vis_dec), (dec_in, dec), (total_in, total))
+        )
+    ]
+    for move in moves:
+        move.start()
+    for move in moves:
+        move.wait()
+    placed = dot(pick[...], vis_dec[...], TN)
+    seen = dot(pick[...], jnp.ones((CAP, 128), BF16), TN)
+    for lane in range(0, DEC, 128):
+        at = slice(lane, lane + 128)
+        old = dec[:, at].astype(F32)
+        decoded_out[:, at] = jnp.where(seen > 0.5, placed[:, at], old).astype(BF16)
+    grad_out[...] = total[...]
 
 
 def shards(
@@ -638,14 +664,16 @@
     vmem = pl.BlockSpec(memory_space=pltpu.VMEM)
     hbm = pl.BlockSpec(memory_space=pl.ANY)
     dma = pltpu.SemaphoreType.DMA
-    decoded, grad = pl.pallas_call(
+    parts = pl.pallas_call(
         kernel,
         out_shape=(
             jax.ShapeDtypeStruct((TOK, DEC), BF16),
+            jax.ShapeDtypeStruct((CAP, DEC), BF16),
+            jax.ShapeDtypeStruct((CAP, TOK), BF16),
             jax.ShapeDtypeStruct((DEC // N, PIX), F32),
         ),
         in_specs=[hbm, vmem, vmem, vmem, vmem, vmem, vmem, hbm, vmem, vmem, vmem, hbm, hbm],
-        out_specs=(vmem, vmem),
+        out_specs=(vmem, vmem, vmem, vmem),
         scratch_shapes=[
             pltpu.VMEM((TOK, D), BF16),
             pltpu.VMEM((TOK, DEC), BF16),
@@ -712,6 +740,23 @@
         w_pixel.T,
         target[0].T,
     )
+    decoded, grad = pl.pallas_call(
+        merge,
+        out_shape=(
+            jax.ShapeDtypeStruct((TOK, DEC), BF16),
+            jax.ShapeDtypeStruct((DEC // N, PIX), F32),
+        ),
+        in_specs=[hbm] * 4,
+        out_specs=(vmem, vmem),
+        scratch_shapes=[
+            pltpu.VMEM((TOK, DEC), BF16),
+            pltpu.VMEM((CAP, DEC), BF16),
+            pltpu.VMEM((CAP, TOK), BF16),
+            pltpu.VMEM((DEC // N, PIX), F32),
+            dma((4,)),
+        ],
+        compiler_params=pltpu.CompilerParams(vmem_limit_bytes=60 * 1024 * 1024),
+    )(*parts)
     return decoded[None], grad[None]
 
 

time: 83 us -> 80.1 us (0.965); the launches traced: 82.8 us -> 78.9 us
  local copies, waits for them, and re-layouts: 3.56 us -> 0 us
    unnamed x2 -> x0, local copies, waits for them, and re-layouts: 3.56 us -> none
    pallas_call x1, Pallas kernels: 78.6 us -> 75.4 us  [shards(): pl.pallas_call(kernel, out_shape=(jax.ShapeDtypeStruct((TOK, DEC), BF16),...]
    pallas_call x0 -> x1, Pallas kernels: none -> 2.67 us  [shards(): pl.pallas_call(merge, out_shape=(jax.ShapeDtypeStruct((TOK, DEC), BF16),...]
where the time goes in v1:
time: 80.1 us; the launch traced here: 78.9 us
  Pallas kernels  78.1 us (98%)
    pallas_call x1, Pallas kernels, shards(): pl.pallas_call(kernel, out_shape=(jax.ShapeDtypeStruct((TOK, DEC), BF16),...  75.4 us
    pallas_call x1, Pallas kernels, shards(): pl.pallas_call(merge, out_shape=(jax.ShapeDtypeStruct((TOK, DEC), BF16),...  2.67 us

profile of v1, /device:TPU:1, one launch (start us, length us, event | category | flops | bytes accessed | tf_op | source)
XLA Modules:
  0.0 78.9 jit_solution(10952619264904689666)
XLA Ops:
  0.6 75.4 %shard_map.140 = (bf16[640,512]{1,0:T(8,128)(2,1)}, bf16[128,512]{1,0:T(8,128)(2,1)}, bf16[128,640]{1,0:T(8,128)(2,1)}, f32[32,1176]{1,0:T(8,128)}) custom-call(bf16[640,1408]{1,0:T(8,128)(2,1)} %bitcast.10, s32[1,1024]{1,0:T(1,128)} %vis.1, f32[1408]{0:T(1024)} %enc_gain.1, bf16[3,88,1408]{2,1,0:T(8,128)(2,1)} %bitcast.13, bf16[88,1408]{1,0:T(8,128)(2,1)} %w_out.1, ...), custom_call_target="tpu_custom_call" | custom-call | tf_op jit(solution)/shard_map/pallas_call | solution.py:667
  76.0 2.7 %shard_map.141 = (bf16[640,512]{1,0:T(8,128)(2,1)}, f32[32,1176]{1,0:T(8,128)}) custom-call(bf16[640,512]{1,0:T(8,128)(2,1)} %get-tuple-element.8.dec_in, bf16[128,512]{1,0:T(8,128)(2,1)} %get-tuple-element.9.vis_in, bf16[128,640]{1,0:T(8,128)(2,1)} %get-tuple-element.10.pick_in, f32[32,1176]{1,0:T(8,128)} %get-tuple-element.11.total_in), custom_call_target="tpu_custom_call" | custom-call | tf_op jit(solution)/shard_map/pallas_call | solution.py:743
